TPU v7x, 32 devices: a whole 2x2x4 slice. The times are simulated.
32 devices in a mesh: seq: 8 (over z, x), kvh: 4 (over y, core).
Axes of the slice: x: 2, y: 2, z: 4, core: 2. Of those that a mesh axis runs over, the one named last changes fastest.
Arguments:
- queries: bfloat16 [4096, 4, 4, 128], P('seq', 'kvh'), may hold values from -12 to 12
- key_states: bfloat16 [4096, 4, 128], P('seq', 'kvh'), may hold values from -10 to 10
- value_states: bfloat16 [4096, 4, 128], P('seq', 'kvh'), may hold values from -4 to 4
- grad_out: bfloat16 [4096, 4, 4, 128], P('seq', 'kvh'), may hold values from -96 to 96
- ancestors: int32 [8, 6], replicated, may hold values from -1 to 6, as said below
- query_weight: bfloat16 [8192, 4, 4, 128], P(None, 'kvh'), may hold values from -0.0625 to 0.0625
- key_weight: bfloat16 [8192, 4, 128], P(None, 'kvh'), may hold values from -0.0625 to 0.0625
- value_weight: bfloat16 [8192, 4, 128], P(None, 'kvh'), may hold values from -0.0625 to 0.0625
Outputs:
- grad_input: bfloat16 [4096, 8192], P(('seq', 'kvh'))
- grad_key: bfloat16 [4096, 4, 128], P('seq', 'kvh')
- grad_value: bfloat16 [4096, 4, 128], P('seq', 'kvh')
Inputs may be any that keep to these rules, and one draw needn't show every extreme that they name: Row b lists the strict ancestor blocks of block b, the root block 0 in slot 0 and one level deeper in each further slot, all below b; the remaining slots hold -1. Block 0 has no ancestors and is an ancestor of every other block; the blocks of every subtree are consecutive; some block has 6 ancestors.
All inputs are finite; a program needn't handle non-finite values.
Results may differ from a plain program's by a relative error of at most 0.015.
Values may be sent and summed in bfloat16 or wider, within the bound.
A program may use at most 128 MiB of HBM per device.

v0:
```python
import jax
import jax.numpy as jnp
from jax import lax
from jax.sharding import PartitionSpec as P

BLOCK = 512
DEPTH = 6


def score_block(query_block, key_block, factor):
    return (
        jnp.einsum("qgd,kd->gqk", query_block, key_block, preferred_element_type=jnp.float32)
        * factor
    )


def local(
    queries, key_states, value_states, grad_out, ancestors, query_weight, key_weight, value_weight
):
    local_rows = queries.shape[0]
    head_count = queries.shape[2]
    head_width = queries.shape[3]
    factor = head_width ** (-0.5)
    query_local = queries[:, 0]
    grad_local = grad_out[:, 0]
    pair_local = jnp.concatenate([key_states, value_states], 1)
    gathered = lax.all_gather(pair_local, "seq", axis=0, tiled=True)
    window = gathered.shape[0]
    block_count = local_rows // BLOCK
    first_block = lax.axis_index("seq") * block_count
    offsets = jnp.arange(BLOCK, dtype=jnp.int32)
    causal = (offsets[:, None] >= offsets[None, :])[None]
    carried = (jnp.zeros((window, 2, head_width), jnp.float32),)

    def deposit(carried, target, contribution):
        row_base = target * BLOCK
        current = lax.dynamic_slice_in_dim(carried[0], row_base, BLOCK, 0)
        return (lax.dynamic_update_slice_in_dim(carried[0], current + contribution, row_base, 0),)

    depth_list = []
    block_id = first_block + 0
    query_block = query_local
    grad_block = grad_local
    listed = lax.dynamic_index_in_dim(ancestors, block_id, 0, keepdims=False)
    depth_here = jnp.sum((listed >= 0).astype(jnp.int32))
    depth_list.append(depth_here)
    slot_total = DEPTH

    def fetch_slot(slot_id, listed=listed):
        target = lax.dynamic_index_in_dim(listed, slot_id, 0, keepdims=False)
        present = target >= 0
        anchor = jnp.maximum(target, 0)
        pair_block = lax.dynamic_slice_in_dim(gathered, anchor * BLOCK, BLOCK, 0)
        return (anchor, present, pair_block)

    def gather_stats(running, pair_block, visible, query_block=query_block, grad_block=grad_block):
        row_peak, total_mass, weighted = running
        scores = jnp.where(visible, score_block(query_block, pair_block[:, 0], factor), -jnp.inf)
        new_peak = jnp.maximum(row_peak, jnp.max(scores, axis=-1, keepdims=True))
        rescale = jnp.exp(row_peak - new_peak)
        exp_terms = jnp.where(visible, jnp.exp(scores - new_peak), 0.0)
        grad_probs = jnp.einsum(
            "qgd,kd->gqk", grad_block, pair_block[:, 1], preferred_element_type=jnp.float32
        )
        total_mass = total_mass * rescale + jnp.sum(exp_terms, axis=-1, keepdims=True)
        weighted = weighted * rescale + jnp.sum(exp_terms * grad_probs, axis=-1, keepdims=True)
        return (new_peak, total_mass, weighted)

    def stats_step(slot_id, running, fetch_slot=fetch_slot, gather_stats=gather_stats):
        anchor, present, pair_block = fetch_slot(slot_id)
        return gather_stats(running, pair_block, present)

    running = (
        jnp.full((head_count, BLOCK, 1), -jnp.inf, jnp.float32),
        jnp.zeros((head_count, BLOCK, 1), jnp.float32),
        jnp.zeros((head_count, BLOCK, 1), jnp.float32),
    )
    running = gather_stats(running, pair_local, causal)
    running = lax.fori_loop(0, slot_total, stats_step, running)
    log_norm = running[0] + jnp.log(running[1])
    delta_row = running[2] / running[1]

    def backward_terms(
        pair_block,
        visible,
        query_block=query_block,
        grad_block=grad_block,
        log_norm=log_norm,
        delta_row=delta_row,
    ):
        scores = score_block(query_block, pair_block[:, 0], factor)
        attn_weight = jnp.where(visible, jnp.exp(scores - log_norm), 0.0)
        grad_probs = jnp.einsum(
            "qgd,kd->gqk", grad_block, pair_block[:, 1], preferred_element_type=jnp.float32
        )
        grad_scores = (attn_weight * (grad_probs - delta_row) * factor).astype(jnp.bfloat16)
        prob_low = attn_weight.astype(jnp.bfloat16)
        query_term = jnp.einsum(
            "gqk,kd->qgd", grad_scores, pair_block[:, 0], preferred_element_type=jnp.float32
        )
        key_term = jnp.einsum(
            "gqk,qgd->kd", grad_scores, query_block, preferred_element_type=jnp.float32
        )
        value_term = jnp.einsum(
            "gqk,qgd->kd", prob_low, grad_block, preferred_element_type=jnp.float32
        )
        return (query_term, jnp.stack([key_term, value_term], 1))

    def grad_step(slot_id, loop_carry, fetch_slot=fetch_slot, backward_terms=backward_terms):
        query_total, inner_carried = loop_carry
        anchor, present, pair_block = fetch_slot(slot_id)
        query_term, pair_term = backward_terms(pair_block, present)
        return (query_total + query_term, deposit(inner_carried, anchor, pair_term))

    query_total, pair_term = backward_terms(pair_local, causal)
    carried = deposit(carried, block_id, pair_term)
    query_total, carried = lax.fori_loop(0, slot_total, grad_step, (query_total, carried))
    query_parts = query_total.astype(jnp.bfloat16)
    pair_grads = lax.psum_scatter(
        carried[0].astype(jnp.bfloat16), "seq", scatter_dimension=0, tiled=True
    )
    flat_query = query_parts.reshape(local_rows, head_count * head_width)
    query_matrix = query_weight[:, 0].reshape(query_weight.shape[0], head_count * head_width)
    key_matrix = key_weight[:, 0]
    value_matrix = value_weight[:, 0]
    contract = (((1,), (1,)), ((), ()))
    key_rows = pair_grads[:, 0]
    value_rows = pair_grads[:, 1]
    result = lax.dot_general(flat_query, query_matrix, contract, preferred_element_type=jnp.float32)
    result = result + lax.dot_general(
        key_rows, key_matrix, contract, preferred_element_type=jnp.float32
    )
    grad_input = lax.psum_scatter(
        (
            result
            + lax.dot_general(
                value_rows, value_matrix, contract, preferred_element_type=jnp.float32
            )
        ).astype(jnp.bfloat16),
        "kvh",
        scatter_dimension=0,
        tiled=True,
    )
    return (grad_input, pair_grads[:, 0:1], pair_grads[:, 1:2])


def solution(mesh):
    return jax.shard_map(
        local,
        mesh=mesh,
        in_specs=(
            P("seq", "kvh", None, None),
            P("seq", "kvh", None),
            P("seq", "kvh", None),
            P("seq", "kvh", None, None),
            P(),
            P(None, "kvh", None, None),
            P(None, "kvh", None),
            P(None, "kvh", None),
        ),
        out_specs=(P(("seq", "kvh"), None), P("seq", "kvh", None), P("seq", "kvh", None)),
        check_vma=False,
    )
```

profile of v0, /device:TPU:0, one launch (start us, length us, event | category | flops | bytes accessed | tf_op | source)
XLA Modules:
  0.0 359.8 jit_solution(15568833139301307411)
XLA Ops:
  12.0 3.6 %fusion.30 = (f32[4,512]{1,0:T(4,128)S(1)}, f32[4,512]{1,0:T(4,128)S(1)}, f32[512,512,4]{1,0,2:T(8,128)}) fusion(f32[512,512,4]{1,0,2:T(8,128)S(1)} %get-tuple-element.360, f32[4,512]{1,0:T(4,128)S(1)} %get-tuple-element.359, pred[512,512]{0,1:T(8,128)(4,1)S(1)} %iota_compare_fusion, bf16[512,1,4,128]{3,2,1,0:T(4,128)(2,1)S(1)} %copy-done.10, ...), kind=kOutput, calls=%fused_computation.47 | convolution fusion | flops 275771392 | bytes 9330688 | tf_op jit(solution)/shard_map/qgd,kd->gqk/dot_general | solution.py:62
  16.6 46.2 %all-gather.2.cloned.1.call-done = bf16[4096,2,128]{2,0,1:T(8,128)(2,1)} async-done(((bf16[512,2,128]{2,0,1:T(8,128)(2,1)}), bf16[4096,2,128]{2,0,1:T(8,128)(2,1)}) %all-gather.2.cloned.1.call-update) | async-done | bytes 2097168 | tf_op jit(solution)/shard_map/all_gather | solution.py:27
  62.8 41.1 %while.32 = (s32[]{:T(128)}, f32[4,512,1]{1,0,2:T(4,128)S(1)}, f32[4,512,1]{1,0,2:T(4,128)S(1)}, f32[4,512,1]{1,0,2:T(4,128)S(1)}, s32[6]{0:T(128)S(1)}, /*index...) while((s32[]{:T(128)}, f32[4,512,1]{1,0,2:T(4,128)S(1)}, ...), condition=%wide.region_7.8_spmd, body=%wide.region_3.7_spmd.sunk | while | flops 551557120 | bytes 16140049 | solution.py:79
  103.9 4.1 %fusion.45 = f32[512,1,128]{2,0,1:T(8,128)} fusion(f32[512,512,4]{1,0,2:T(8,128)} %copy-done.4, f32[4,512]{1,0:T(4,128)S(1)} %bitcast.256, pred[512,512]{0,1:T(8,128)(4,1)S(1)} %iota_compare_fusion, bf16[512,1,4,128]{3,2,1,0:T(4,128)(2,1)} %param.15), kind=kOutput, calls=%fused_computation.65 | convolution fusion | flops 272629760 | bytes 5251072 | tf_op jit(solution)/shard_map/gqk,qgd->kd/dot_general | solution.py:104
  108.0 3.6 fusion.33
  114.7 2.6 copy.16
  120.2 66.6 %while.33 = (s32[]{:T(128)}, f32[512,4,128]{0,2,1:T(8,128)}, f32[4096,2,128]{2,0,1:T(8,128)}, s32[6]{0:T(128)S(1)}, bf16[4096,2,128]{2,0,1:T(8,128)(2,1)}, /*ind...) while((s32[]{:T(128)}, f32[512,4,128]{0,2,1:T(8,128)}, ...), condition=%wide.region_9.10_spmd, body=%wide.region_8.9_spmd.sunk | while | flops 1354235904 | bytes 33973052 | solution.py:117
  124.6 2.4 fusion.97
  129.0 2.3 fusion.100
  135.6 2.4 fusion.97
  140.2 2.3 fusion.100
  146.8 2.4 fusion.97
  151.2 2.3 fusion.100
  157.8 2.4 fusion.97
  162.3 2.3 fusion.100
  168.9 2.4 fusion.97
  173.4 2.3 fusion.100
  180.0 2.4 fusion.97
  186.8 3.8 %convert_element_type.32 = bf16[4096,2,128]{2,0,1:T(8,128)(2,1)} convert(f32[4096,2,128]{2,0,1:T(8,128)} %get-tuple-element.303) | non-fusion elementwise | flops 1048576 | bytes 6291456 | tf_op jit(solution)/shard_map/convert_element_type | solution.py:120
  192.0 11.8 %fusion.27 = f32[512,8192]{1,0:T(8,128)} fusion(bf16[512,512]{0,1:T(8,128)(2,1)S(1)} %bitcast.254, bf16[1024,8,4,128]{3,2,1,0:T(4,128)(2,1)} %bitcast.251), kind=kOutput, calls=%fused_computation.42 | convolution fusion | flops 4294967296 | bytes 25690112 | tf_op jit(solution)/shard_map/dot_general | solution.py:129
  203.8 53.6 %reduce-scatter.3.cloned.1.call-done = bf16[512,2,128]{2,0,1:T(8,128)(2,1)} async-done(((bf16[4096,2,128]{2,0,1:T(8,128)(2,1)}), bf16[512,2,128]{2,0,1:T(8,128)(2,1)}) %reduce-scatter.3.cloned.1.call-update) | async-done | bytes 262160 | tf_op jit(solution)/shard_map/reduce_scatter | solution.py:119
  258.4 8.1 %fusion.40 = f32[512,8192]{1,0:T(8,128)} fusion(bf16[8192,1,128]{2,0,1:T(8,128)(2,1)S(1)} %copy-done, bf16[512,1,128]{2,0,1:T(8,128)(2,1)S(1)} %get-tuple-element.354), kind=kOutput, calls=%fused_computation.60 | convolution fusion | flops 1073741824 | bytes 19005440 | tf_op jit(solution)/shard_map/dot_general | solution.py:130
  266.5 15.9 %add_convert_fusion = bf16[512,8192]{1,0:T(8,128)(2,1)} fusion(f32[512,8192]{1,0:T(8,128)} %fusion.27, f32[512,8192]{1,0:T(8,128)} %fusion.40, bf16[8192,1,128]{2,0,1:T(8,128)(2,1)} %param.19, bf16[512,1,128]{2,0,1:T(8,128)(2,1)S(1)} %get-tuple-element.353), kind=kOutput, calls=%fused_computation.41 | convolution fusion | flops 1086324736 | bytes 44171264 | tf_op jit(solution)/shard_map/dot_general | solution.py:136
  282.4 70.9 %reduce-scatter.5.cloned.1.call-done = bf16[128,8192]{1,0:T(8,128)(2,1)} async-done(((bf16[512,8192]{1,0:T(8,128)(2,1)}), bf16[128,8192]{1,0:T(8,128)(2,1)}) %reduce-scatter.5.cloned.1.call-update) | async-done | bytes 2097168 | tf_op jit(solution)/shard_map/reduce_scatter | solution.py:133
  (156 shorter events, 79.5 us)
Async XLA Ops:
  7.2 251.2 %copy-start = (bf16[8192,1,128]{2,0,1:T(8,128)(2,1)S(1)}, bf16[8192,1,128]{2,0,1:T(8,128)(2,1)}, u32[]{:S(2)}) copy-start(bf16[8192,1,128]{2,0,1:T(8,128)(2,1)} %param.18) | copy-start | bytes 6291460
  7.2 4.8 %copy-start.16 = (bf16[512,1,128]{2,0,1:T(8,128)(2,1)S(1)}, bf16[512,1,128]{2,0,1:T(8,128)(2,1)}, u32[]{:S(2)}) copy-start(bf16[512,1,128]{2,0,1:T(8,128)(2,1)} %param.14) | copy-start | bytes 393220
  7.2 4.8 %copy-start.10 = (bf16[512,1,4,128]{3,2,1,0:T(4,128)(2,1)S(1)}, bf16[512,1,4,128]{3,2,1,0:T(4,128)(2,1)}, u32[]{:S(2)}) copy-start(bf16[512,1,4,128]{3,2,1,0:T(4,128)(2,1)} %param.15) | copy-start | bytes 1572868
  7.2 55.6 %all-gather.2.cloned.1.call-start = ((), (), s32[]{:S(2)}) async-start(), calls=%async_computation.2 | async-start | bytes 2359296 | tf_op jit(solution)/shard_map/all_gather | solution.py:27
  9.1 248.3 %reduce-scatter.3.cloned.1.call-start = ((), (), s32[]{:S(2)}) async-start(), calls=%async_computation.3 | async-start | bytes 2359296 | tf_op jit(solution)/shard_map/reduce_scatter | solution.py:119
  12.0 3.7 %copy-start.4 = (f32[512,512,4]{1,0,2:T(8,128)}, f32[512,512,4]{1,0,2:T(8,128)S(1)}, u32[]{:S(2)}) copy-start(f32[512,512,4]{1,0,2:T(8,128)S(1)} %get-tuple-element.360) | copy-start | bytes 12582916
  12.0 3.7 %copy-start.6 = (bf16[512,1,4,128]{3,2,1,0:T(4,128)(2,1)S(1)}, bf16[512,1,4,128]{3,2,1,0:T(4,128)(2,1)}, u32[]{:S(2)}) copy-start(bf16[512,1,4,128]{3,2,1,0:T(4,128)(2,1)} %param.12) | copy-start | bytes 1572868
  12.0 3.7 %copy-start.11 = (bf16[512,1,4,128]{3,2,1,0:T(4,128)(2,1)S(1)}, bf16[512,1,4,128]{3,2,1,0:T(4,128)(2,1)}, u32[]{:S(2)}) copy-start(bf16[512,1,4,128]{3,2,1,0:T(4,128)(2,1)} %param.15) | copy-start | bytes 1572868
  64.0 2.4 copy-start.12
  77.7 2.4 copy-start.12
  91.4 2.4 copy-start.12
  103.9 4.1 %copy-start.5 = (f32[512,512,4]{1,0,2:T(8,128)S(1)}, f32[512,512,4]{1,0,2:T(8,128)}, u32[]{:S(2)}) copy-start(f32[512,512,4]{1,0,2:T(8,128)} %copy-done.4) | copy-start | bytes 12582916
  108.0 5.0 %copy-start.7 = (bf16[512,1,128]{2,0,1:T(8,128)(2,1)S(1)}, bf16[512,1,128]{2,0,1:T(8,128)(2,1)}, u32[]{:S(2)}) copy-start(bf16[512,1,128]{2,0,1:T(8,128)(2,1)} %param.13) | copy-start | bytes 393220
  113.0 4.6 %copy-start.14 = (f32[512,1,128]{2,0,1:T(8,128)S(1)}, f32[512,1,128]{2,0,1:T(8,128)}, u32[]{:S(2)}) copy-start(f32[512,1,128]{2,0,1:T(8,128)} %fusion.45) | copy-start | bytes 786436
  114.7 5.6 %copy-start.13 = (bf16[512,4,128]{2,0,1:T(8,128)(2,1)S(1)}, bf16[512,4,128]{2,0,1:T(8,128)(2,1)}, u32[]{:S(2)}) copy-start(bf16[512,4,128]{2,0,1:T(8,128)(2,1)} %get-tuple-element.575) | copy-start | bytes 1572868
  124.5 3.1 copy-start.1
  135.6 3.1 copy-start.1
  146.7 3.1 copy-start.1
  157.8 3.1 copy-start.1
  168.9 3.1 copy-start.1
  180.0 3.1 copy-start.1
  190.6 162.6 %reduce-scatter.5.cloned.1.call-start = ((), (), s32[]{:S(2)}) async-start(), calls=%async_computation.4 | async-start | bytes 10485760 | tf_op jit(solution)/shard_map/reduce_scatter | solution.py:133
  258.4 8.1 %copy-start.9 = (bf16[512,1,128]{2,0,1:T(8,128)(2,1)}, bf16[512,1,128]{2,0,1:T(8,128)(2,1)S(1)}, u32[]{:S(2)}) copy-start(bf16[512,1,128]{2,0,1:T(8,128)(2,1)S(1)} %get-tuple-element.354) | copy-start | bytes 393220
  258.4 8.1 %copy-start.8 = (bf16[512,1,128]{2,0,1:T(8,128)(2,1)}, bf16[512,1,128]{2,0,1:T(8,128)(2,1)S(1)}, u32[]{:S(2)}) copy-start(bf16[512,1,128]{2,0,1:T(8,128)(2,1)S(1)} %get-tuple-element.353) | copy-start | bytes 393220
  (11 other events, 23.8 us)
Sparse Core Ops, SparseCore 0:
  10.8 51.9 all-gather.1
  190.8 66.5 reduce-scatter.2
  282.5 70.7 reduce-scatter.4
where the time goes:
time: 361 us; the launch traced here: 360 us
  waiting for transfers between devices  171 us (47%)
  matrix products  113 us (31%)
  other arithmetic  30.4 us (8%)
  loops' own time  16.7 us (5%)
  local copies, waits for them, and re-layouts  15.3 us (4%)
  between operations  13.9 us (4%)
    reduce_scatter x1, waiting for transfers between devices, local(): lax.psum_scatter((result + lax.dot_general(value_rows, value_matrix, cont...  70.9 us
    reduce_scatter x1, waiting for transfers between devices, local(): lax.psum_scatter(carried[0].astype(jnp.bfloat16), 'seq', scatter_dimensio...  53.6 us
    all_gather x1, waiting for transfers between devices, local(): gathered = lax.all_gather(pair_local, 'seq', axis=0, tiled=True)  46.2 us
    dot_general x13, matrix products, score_block(): jnp.einsum('qgd,kd->gqk', query_block, key_block, preferred_element_type=...  21.5 us
    dot_general x7, matrix products, gather_stats(): jnp.einsum('qgd,kd->gqk', grad_block, pair_block[:, 1], preferred_element...  16.8 us
    dot_general x1, matrix products, local(): lax.dot_general(value_rows, value_matrix, contract, preferred_element_typ...  15.9 us
    dot_general x6, matrix products, backward_terms(): jnp.einsum('qgd,kd->gqk', grad_block, pair_block[:, 1], preferred_element...  14.2 us
    dynamic_update_slice x7, other arithmetic, deposit(): lax.dynamic_update_slice_in_dim(carried[0], current + contribution, row_b...  13.8 us
  transfers between devices with their start and end apart: 3, of which 3 were waited for; matrix products, arithmetic and copies ran while one was open for 6% of the time, Pallas kernels for 0%

commit v1 on v0

v1 whole, which is shorter than its diff:
```python
import functools

import jax
import jax.numpy as jnp
from jax import lax
from jax.experimental import pallas as pl
from jax.experimental.pallas import tpu as pltpu
from jax.sharding import PartitionSpec as P

BLOCK = 512
WIDTH = 128
HEADS = 4
NT = (((1,), (1,)), ((), ()))
NN = (((1,), (0,)), ((), ()))
TN = (((0,), (0,)), ((), ()))
LOG2E = 1.4426950408889634


def dot(a, b, dims):
    return lax.dot_general(a, b, dims, preferred_element_type=jnp.float32)


def causal_mask():
    keys = lax.broadcasted_iota(jnp.int32, (BLOCK, BLOCK), 0)
    rows = lax.broadcasted_iota(jnp.int32, (BLOCK, BLOCK), 1)
    return keys <= rows


def attention_kernel(vis_ref, q_ref, do_ref, kv_ref, dq_ref, dkv_ref, dq_acc, peak, mass, weighted):
    me = lax.axis_index("seq")
    blocks = kv_ref.shape[0] // BLOCK
    factor = WIDTH ** -0.5

    def rows_of(j):
        return pl.ds(pl.multiple_of(j * BLOCK, BLOCK), BLOCK)

    def stats(j, first):
        keys = kv_ref[rows_of(j), :WIDTH]
        values = kv_ref[rows_of(j), WIDTH:]
        for g in range(HEADS):
            lanes = slice(g * WIDTH, (g + 1) * WIDTH)
            scores = dot(keys, q_ref[:, lanes], NT) * (factor * LOG2E)
            if first:
                scores = jnp.where(causal_mask(), scores, -jnp.inf)
            grads = dot(values, do_ref[:, lanes], NT)
            top = jnp.max(scores, axis=0, keepdims=True)
            if not first:
                old = peak[g]
                top = jnp.maximum(top, old)
            terms = jnp.exp2(scores - top)
            total = jnp.sum(terms, axis=0, keepdims=True)
            moved = jnp.sum(terms * grads, axis=0, keepdims=True)
            if not first:
                scale = jnp.exp2(old - top)
                total = total + mass[g] * scale
                moved = moved + weighted[g] * scale
            peak[g] = top
            mass[g] = total
            weighted[g] = moved

    def backward(j, first):
        keys = kv_ref[rows_of(j), :WIDTH]
        values = kv_ref[rows_of(j), WIDTH:]
        key_grad = jnp.zeros((BLOCK, WIDTH), jnp.float32)
        value_grad = jnp.zeros((BLOCK, WIDTH), jnp.float32)
        for g in range(HEADS):
            lanes = slice(g * WIDTH, (g + 1) * WIDTH)
            q = q_ref[:, lanes]
            do = do_ref[:, lanes]
            scores = dot(keys, q, NT) * (factor * LOG2E)
            probs = jnp.exp2(scores - peak[g])
            if first:
                probs = jnp.where(causal_mask(), probs, 0.0)
            grads = dot(values, do, NT)
            dscores = (probs * ((grads - weighted[g]) * factor)).astype(jnp.bfloat16)
            value_grad = value_grad + dot(probs.astype(jnp.bfloat16), do, NN)
            key_grad = key_grad + dot(dscores, q, NN)
            term = dot(dscores, keys, TN)
            if first:
                dq_acc[:, lanes] = term
            else:
                dq_acc[:, lanes] += term
        dkv_ref[rows_of(j), :WIDTH] = key_grad.astype(jnp.bfloat16)
        dkv_ref[rows_of(j), WIDTH:] = value_grad.astype(jnp.bfloat16)

    stats(me, True)

    def stats_step(j, carry):
        @pl.when(vis_ref[j] > 0)
        def _():
            stats(j, False)

        return carry

    lax.fori_loop(0, me, stats_step, 0)
    for g in range(HEADS):
        weighted[g] = weighted[g] / mass[g]
        peak[g] = peak[g] + jnp.log2(mass[g])
    backward(me, True)

    def grad_step(j, carry):
        seen = (vis_ref[j] > 0) & (j < me)

        @pl.when(seen)
        def _():
            backward(j, False)

        @pl.when(jnp.logical_not(seen) & (j != me))
        def _():
            dkv_ref[rows_of(j), :] = jnp.zeros((BLOCK, 2 * WIDTH), jnp.bfloat16)

        return carry

    lax.fori_loop(0, blocks, grad_step, 0)
    dq_ref[...] = dq_acc[...].astype(jnp.bfloat16)


def attention(visible, q, do, kv):
    window = kv.shape[0]
    vmem = pl.BlockSpec(memory_space=pltpu.VMEM)
    pairs = HEADS * BLOCK * BLOCK * 7
    return pl.pallas_call(
        attention_kernel,
        out_shape=(
            jax.ShapeDtypeStruct((BLOCK, HEADS * WIDTH), jnp.bfloat16),
            jax.ShapeDtypeStruct((window, 2 * WIDTH), jnp.bfloat16),
        ),
        in_specs=[pl.BlockSpec(memory_space=pltpu.SMEM), vmem, vmem, vmem],
        out_specs=(vmem, vmem),
        scratch_shapes=[
            pltpu.VMEM((BLOCK, HEADS * WIDTH), jnp.float32),
            pltpu.VMEM((HEADS, 1, BLOCK), jnp.float32),
            pltpu.VMEM((HEADS, 1, BLOCK), jnp.float32),
            pltpu.VMEM((HEADS, 1, BLOCK), jnp.float32),
        ],
        compiler_params=pltpu.CompilerParams(vmem_limit_bytes=48 * 2**20),
        cost_estimate=pl.CostEstimate(
            flops=7 * 2 * pairs * WIDTH, bytes_accessed=6 * 2**20, transcendentals=2 * pairs
        ),
        name="attention",
    )(visible, q, do, kv)


def project_kernel(
    size, chunks, dq_ref, dkv_ref, wq_ref, wk_ref, wv_ref, out_ref,
    rows_all, weights, product, own, core_out, core_in, far_out, far_in,
    w_sem, core_send, core_recv, far_send, far_recv,
):
    me = lax.axis_index("kvh")
    layer = me // 2
    core = me % 2
    layers = size // 2
    rows = BLOCK // size
    width = wq_ref.shape[0] // chunks
    qw = HEADS * WIDTH
    peer = layer * 2 + 1 - core

    def weight_copies(i):
        at = pl.ds(pl.multiple_of(i * width, width), width)
        return [
            pltpu.make_async_copy(wq_ref.at[at, :], weights.at[i, :, pl.ds(0, qw)], w_sem.at[i, 0]),
            pltpu.make_async_copy(wk_ref.at[at, :], weights.at[i, :, pl.ds(qw, WIDTH)], w_sem.at[i, 1]),
            pltpu.make_async_copy(
                wv_ref.at[at, :], weights.at[i, :, pl.ds(qw + WIDTH, WIDTH)], w_sem.at[i, 2]
            ),
        ]

    def start_weights(i, carry):
        for copy in weight_copies(i):
            copy.start()
        return carry

    lax.fori_loop(0, chunks, start_weights, 0)
    barrier = pltpu.get_barrier_semaphore()
    far = [lax.rem(layer + d, layers) for d in range(layers)]
    pl.semaphore_signal(barrier, inc=1, device_id={"kvh": peer}, device_id_type=pl.DeviceIdType.MESH)
    for d in range(1, layers):
        pl.semaphore_signal(
            barrier, inc=1, device_id={"kvh": far[d] * 2 + core}, device_id_type=pl.DeviceIdType.MESH
        )
    rows_all[:, :qw] = dq_ref[...]
    rows_all[:, qw:] = dkv_ref[...]
    pl.semaphore_wait(barrier, layers)

    def core_copy(d, i):
        return pltpu.make_async_remote_copy(
            core_out.at[d, i], core_in.at[d, i], core_send.at[d, i], core_recv.at[d, i],
            device_id={"kvh": peer}, device_id_type=pl.DeviceIdType.MESH,
        )

    def far_copy(d, i):
        return pltpu.make_async_remote_copy(
            far_out.at[d - 1, i], far_in.at[d - 1, i], far_send.at[d - 1, i], far_recv.at[d - 1, i],
            device_id={"kvh": far[d] * 2 + core}, device_id_type=pl.DeviceIdType.MESH,
        )

    def part(d, which):
        return pl.ds(pl.multiple_of((far[d] * 2 + which) * rows, rows), rows)

    def begin(i):
        for copy in weight_copies(i):
            copy.wait()
        slot = i % 2
        product[slot] = dot(rows_all[...], weights[i], NT)
        for d in list(range(1, layers)) + [0]:
            core_out[d, i] = product[slot, part(d, 1 - core), :].astype(jnp.bfloat16)
            core_copy(d, i).start()

    def forward(i):
        slot = i % 2
        for d in range(1, layers):
            core_copy(d, i).wait_recv()
            far_out[d - 1, i] = (
                product[slot, part(d, core), :] + core_in[d, i].astype(jnp.float32)
            ).astype(jnp.bfloat16)
            far_copy(d, i).start()
        own[i] = product[slot, part(0, core), :]

    begin(0)

    def step(i, carry):
        begin(i)
        forward(i - 1)
        return carry

    lax.fori_loop(1, chunks, step, 0)
    forward(chunks - 1)

    def finish(i, carry):
        core_copy(0, i).wait_recv()
        total = own[i] + core_in[0, i].astype(jnp.float32)
        for d in range(1, layers):
            far_copy(d, i).wait_recv()
            total = total + far_in[d - 1, i].astype(jnp.float32)
        out_ref[:, pl.ds(pl.multiple_of(i * width, width), width)] = total.astype(jnp.bfloat16)
        for d in range(layers):
            core_copy(d, i).wait_send()
        for d in range(1, layers):
            far_copy(d, i).wait_send()
        return carry

    lax.fori_loop(0, chunks, finish, 0)


def project(size, dq, dkv, wq, wk, wv):
    model = wq.shape[0]
    rows = BLOCK // size
    layers = size // 2
    chunks = 16
    width = model // chunks
    vmem = pl.BlockSpec(memory_space=pltpu.VMEM)
    hbm = pl.BlockSpec(memory_space=pl.ANY)
    full = (HEADS + 2) * WIDTH
    return pl.pallas_call(
        functools.partial(project_kernel, size, chunks),
        out_shape=jax.ShapeDtypeStruct((rows, model), jnp.bfloat16),
        in_specs=[vmem, vmem, hbm, hbm, hbm],
        out_specs=vmem,
        scratch_shapes=[
            pltpu.VMEM((BLOCK, full), jnp.bfloat16),
            pltpu.VMEM((chunks, width, full), jnp.bfloat16),
            pltpu.VMEM((2, BLOCK, width), jnp.float32),
            pltpu.VMEM((chunks, rows, width), jnp.float32),
            pltpu.VMEM((layers, chunks, rows, width), jnp.bfloat16),
            pltpu.VMEM((layers, chunks, rows, width), jnp.bfloat16),
            pltpu.VMEM((layers - 1, chunks, rows, width), jnp.bfloat16),
            pltpu.VMEM((layers - 1, chunks, rows, width), jnp.bfloat16),
            pltpu.SemaphoreType.DMA((chunks, 3)),
            pltpu.SemaphoreType.DMA((layers, chunks)),
            pltpu.SemaphoreType.DMA((layers, chunks)),
            pltpu.SemaphoreType.DMA((layers - 1, chunks)),
            pltpu.SemaphoreType.DMA((layers - 1, chunks)),
        ],
        compiler_params=pltpu.CompilerParams(
            collective_id=1, has_side_effects=True, vmem_limit_bytes=56 * 2**20
        ),
        cost_estimate=pl.CostEstimate(
            flops=2 * BLOCK * full * model, bytes_accessed=2 * full * model, transcendentals=0
        ),
        name="project",
    )(dq, dkv, wq, wk, wv)


def local(
    size, queries, key_states, value_states, grad_out, ancestors, query_weight, key_weight, value_weight
):
    model = query_weight.shape[0]
    q = queries.reshape(BLOCK, HEADS * WIDTH)
    do = grad_out.reshape(BLOCK, HEADS * WIDTH)
    kv = jnp.concatenate([key_states[:, 0], value_states[:, 0]], 1)
    gathered = lax.all_gather(kv, "seq", axis=0, tiled=True)
    blocks = ancestors.shape[0]
    me = lax.axis_index("seq")
    listed = lax.dynamic_index_in_dim(ancestors, me, 0, keepdims=False)
    ids = jnp.arange(blocks, dtype=jnp.int32)
    visible = jnp.any(listed[None, :] == ids[:, None], axis=1).astype(jnp.int32)
    dq, dkv = attention(visible, q, do, gathered)
    pair = lax.psum_scatter(dkv, "seq", scatter_dimension=0, tiled=True)
    grad_input = project(
        size, dq, pair,
        query_weight.reshape(model, HEADS * WIDTH), key_weight[:, 0], value_weight[:, 0],
    )
    return (grad_input, pair[:, None, :WIDTH], pair[:, None, WIDTH:])


def solution(mesh):
    return jax.shard_map(
        functools.partial(local, mesh.shape["kvh"]),
        mesh=mesh,
        in_specs=(
            P("seq", "kvh", None, None),
            P("seq", "kvh", None),
            P("seq", "kvh", None),
            P("seq", "kvh", None, None),
            P(),
            P(None, "kvh", None, None),
            P(None, "kvh", None),
            P(None, "kvh", None),
        ),
        out_specs=(P(("seq", "kvh"), None), P("seq", "kvh", None), P("seq", "kvh", None)),
        check_vma=False,
    )
```

time: 361 us -> 232 us (0.64)
  matrix products: 113 us -> 0 us
  Pallas kernels: 0 us -> 61 us
  waiting for transfers between devices: 171 us -> 139 us
  other arithmetic: 30.4 us -> 1.82 us
  loops' own time: 16.7 us -> 0 us
    dot_general x50 -> x0, matrix products: 113 us -> none  [the longest x13 21.5 us: score_block(): jnp.einsum('qgd,kd->gqk', query_block, key_block, preferred_element_type=...]
    pallas_call x0 -> x2, Pallas kernels: none -> 61 us  [the longest x1 54.2 us: project(): pl.pallas_call(functools.partial(project_kernel, size, chunks), out_shape...]
    reduce_scatter x2 -> x1, waiting for transfers between devices: 124 us -> 86.8 us  [local(): pair = lax.psum_scatter(dkv, 'seq', scatter_dimension=0, tiled=True)]
    another operation x2 -> x0, loops' own time: 16.7 us -> none  [the longest x1 8.55 us: local(): running = lax.fori_loop(0, slot_total, stats_step, running)]
    dynamic_update_slice x7 -> x0, other arithmetic: 13.8 us -> none  [deposit(): lax.dynamic_update_slice_in_dim(carried[0], current + contribution, row_b...]
    unnamed x28 -> x10, local copies, waits for them, and re-layouts: 2.67 us -> 13.6 us
    convert_element_type x3 -> x1, other arithmetic: 8.63 us -> 0.01 us  [local(): visible = jnp.any(listed[None, :] == ids[:, None], axis=1).astype(jnp.int32)]
    dynamic_slice x12 -> x0, local copies, waits for them, and re-layouts: 7.01 us -> none  [fetch_slot(): target = lax.dynamic_index_in_dim(listed, slot_id, 0, keepdims=False)]
  transfers between devices with their start and end apart: 3 -> 2, of which waited for: 3 -> 2; matrix products, arithmetic and copies ran while one was open for 6% -> 4% of each run, Pallas kernels for 0% -> 0%
where the time goes in v1:
time: 232 us
  waiting for transfers between devices  139 us (60%)
  Pallas kernels  61 us (26%)
  local copies, waits for them, and re-layouts  15.7 us (7%)
  between operations  14.1 us (6%)
    reduce_scatter x1, waiting for transfers between devices, local(): pair = lax.psum_scatter(dkv, 'seq', scatter_dimension=0, tiled=True)  86.8 us
    pallas_call x1, Pallas kernels, project(): pl.pallas_call(functools.partial(project_kernel, size, chunks), out_shape...  54.2 us
    all_gather x1, waiting for transfers between devices, local(): gathered = lax.all_gather(kv, 'seq', axis=0, tiled=True)  52.2 us
    unnamed x10, local copies, waits for them, and re-layouts  13.6 us
    pallas_call x1, Pallas kernels, attention(): pl.pallas_call(attention_kernel, out_shape=(jax.ShapeDtypeStruct((BLOCK,...  6.85 us
  transfers between devices with their start and end apart: 2, of which 2 were waited for; matrix products, arithmetic and copies ran while one was open for 4% of the time, Pallas kernels for 0%

profile of v1, /device:TPU:0, one launch (start us, length us, event | category | flops | bytes accessed | tf_op | source)
XLA Modules:
  0.0 231.7 jit_solution(11503162578180601107)
XLA Ops:
  7.2 0.0 copy-start
  7.2 0.0 all-gather.2.cloned.1.call-start
  7.2 1.7 pad_maximum_fusion
  8.9 0.0 all-gather.2.cloned.1.call-update
  9.0 0.0 reduce-scatter.2.cloned.1.call-start
  9.0 0.0 copy-done
  9.0 0.1 fusion
  9.2 1.3 copy_bitcast_fusion.1
  10.5 52.2 %all-gather.2.cloned.1.call-done.kv_ref = bf16[4096,256]{1,0:T(8,128)(2,1)} async-done(((bf16[512,256]{1,0:T(8,128)(2,1)}), bf16[4096,256]{1,0:T(8,128)(2,1)}) %all-gather.2.cloned.1.call-update) | async-done | bytes 2097168 | tf_op jit(solution)/shard_map/all_gather | solution.py:291
  62.7 0.0 copy-start.1
  62.7 1.6 copy-done.1
  64.3 6.8 %attention.1 = (bf16[512,512]{1,0:T(8,128)(2,1)S(1)}, bf16[4096,256]{1,0:T(8,128)(2,1)}) custom-call(s32[8]{0:T(128)S(1)} %convert_element_type.3.vis_ref, bf16[512,512]{1,0:T(8,128)(2,1)S(1)} %get-tuple-element.10.q_ref, bf16[512,512]{1,0:T(8,128)(2,1)S(1)} %get-tuple-element.9.do_ref, bf16[4096,256]{1,0:T(8,128)(2,1)S(1)} %copy-done.1), custom_call_target="tpu_custom_call" | custom-call | flops 13153337344 | bytes 6291456 | tf_op jit(solution)/shard_map/attention/pallas_call | solution.py:122
  71.2 0.0 copy-start.2
  71.2 0.8 copy-done.2
  72.0 0.0 reduce-scatter.2.cloned.1.call-update
  72.0 8.1 %copy.17 = bf16[1024,8,4,128]{3,1,2,0:T(8,128)(2,1)} copy(bf16[1024,8,4,128]{3,2,1,0:T(4,128)(2,1)} %bitcast.23) | data formatting | bytes 16777216
  80.1 86.8 %reduce-scatter.2.cloned.1.call-done.dkv_ref = bf16[512,256]{1,0:T(8,128)(2,1)} async-done(((bf16[4096,256]{1,0:T(8,128)(2,1)}), bf16[512,256]{1,0:T(8,128)(2,1)}) %reduce-scatter.2.cloned.1.call-update) | async-done | bytes 262160 | tf_op jit(solution)/shard_map/reduce_scatter | solution.py:298
  166.9 0.0 copy-start.3
  166.9 54.2 %project.1 = bf16[128,8192]{1,0:T(8,128)(2,1)} custom-call(bf16[512,512]{1,0:T(8,128)(2,1)} %copy-done.2, bf16[512,256]{1,0:T(8,128)(2,1)} %reduce-scatter.2.cloned.1.call-done.dkv_ref, bf16[8192,512]{1,0:T(8,128)(2,1)} %bitcast.24, bf16[8192,128]{1,0:T(8,128)(2,1)} %bitcast.29, bf16[8192,128]{1,0:T(8,128)(2,1)} %bitcast.30), custom_call_target="tpu_custom_call" | custom-call | flops 6442450944 | bytes 12582912 | tf_op jit(solution)/shard_map/project/pallas_call | solution.py:254
  221.1 0.0 copy-done.3
  221.1 0.7 slice_bitcast_fusion
  221.8 3.1 %copy.19 = bf16[128,8192]{1,0:T(8,128)(2,1)} copy(bf16[128,8192]{1,0:T(8,128)(2,1)} %project.1) | data formatting | bytes 4194304
  (2 shorter events, 0.0 us)
Async XLA Ops:
  7.2 1.8 copy-start
  7.2 55.6 %all-gather.2.cloned.1.call-start = ((), (), s32[]{:S(2)}) async-start(), calls=%async_computation.1 | async-start | bytes 2359296 | tf_op jit(solution)/shard_map/all_gather | solution.py:291
  9.0 158.0 %reduce-scatter.2.cloned.1.call-start = ((), (), s32[]{:S(2)}) async-start(), calls=%async_computation.2 | async-start | bytes 2359296 | tf_op jit(solution)/shard_map/reduce_scatter | solution.py:298
  62.7 1.6 copy-start.1
  71.2 0.8 copy-start.2
  166.9 54.2 %copy-start.3 = (bf16[512,256]{1,0:T(8,128)(2,1)S(1)}, bf16[512,256]{1,0:T(8,128)(2,1)}, u32[]{:S(2)}) copy-start(bf16[512,256]{1,0:T(8,128)(2,1)} %reduce-scatter.2.cloned.1.call-done.dkv_ref) | copy-start | bytes 786436
Sparse Core Ops, SparseCore 0:
  10.7 51.9 all-gather.1
  72.1 94.7 reduce-scatter.1

commit v2 on v1

--- a/solution.py
+++ b/solution.py
@@ -26,17 +26,63 @@
     return keys <= rows
 
 
-def attention_kernel(vis_ref, q_ref, do_ref, kv_ref, dq_ref, dkv_ref, dq_acc, peak, mass, weighted):
+def attention_kernel(
+    columns, bias_ref, q_ref, do_ref, kv_ref, dq_ref, dkv_ref,
+    kv_all, dq_acc, peak, mass, weighted, col, peer_out, peer_in, up_in, up_out,
+    got, z_sent, x_sent, peer_sent, peer_got, up_sent, up_got,
+):
     me = lax.axis_index("seq")
-    blocks = kv_ref.shape[0] // BLOCK
+    blocks = kv_all.shape[0] // BLOCK
+    levels = blocks // columns
+    z = me // columns
+    x = me % columns
     factor = WIDTH ** -0.5
+    mesh_id = pl.DeviceIdType.MESH
+    inner = z < levels - 1
 
     def rows_of(j):
         return pl.ds(pl.multiple_of(j * BLOCK, BLOCK), BLOCK)
 
+    def beside(d):
+        return lax.rem(x + d, columns)
+
+    def before(d):
+        return lax.rem(x + columns - d, columns)
+
+    def z_copy(level):
+        at = rows_of(level * columns + x)
+        return pltpu.make_async_remote_copy(
+            kv_all.at[at, :], kv_all.at[at, :], z_sent.at[level], got.at[level * columns + x],
+            device_id={"seq": me + columns}, device_id_type=mesh_id,
+        )
+
+    def x_copy(level, d):
+        at = rows_of(level * columns + x)
+        return pltpu.make_async_remote_copy(
+            kv_all.at[at, :], kv_all.at[at, :], x_sent.at[level, d - 1], got.at[level * columns + x],
+            device_id={"seq": z * columns + beside(d)}, device_id_type=mesh_id,
+        )
+
+    def wait_block(j):
+        at = rows_of(j)
+        pltpu.make_async_copy(kv_all.at[at, :], kv_all.at[at, :], got.at[j]).wait()
+
+    def peer_copy(level, d):
+        return pltpu.make_async_remote_copy(
+            peer_out.at[level, d - 1], peer_in.at[level, d - 1],
+            peer_sent.at[level, d - 1], peer_got.at[level, d - 1],
+            device_id={"seq": z * columns + beside(d)}, device_id_type=mesh_id,
+        )
+
+    def up_copy(level):
+        return pltpu.make_async_remote_copy(
+            up_out.at[level], up_in.at[level], up_sent.at[level], up_got.at[level],
+            device_id={"seq": me - columns}, device_id_type=mesh_id,
+        )
+
     def stats(j, first):
-        keys = kv_ref[rows_of(j), :WIDTH]
-        values = kv_ref[rows_of(j), WIDTH:]
+        keys = kv_all[rows_of(j), :WIDTH]
+        values = kv_all[rows_of(j), WIDTH:]
         for g in range(HEADS):
             lanes = slice(g * WIDTH, (g + 1) * WIDTH)
             scores = dot(keys, q_ref[:, lanes], NT) * (factor * LOG2E)
@@ -44,10 +90,12 @@
                 scores = jnp.where(causal_mask(), scores, -jnp.inf)
             grads = dot(values, do_ref[:, lanes], NT)
             top = jnp.max(scores, axis=0, keepdims=True)
+            shift = top
             if not first:
                 old = peak[g]
-                top = jnp.maximum(top, old)
-            terms = jnp.exp2(scores - top)
+                top = jnp.maximum(top + bias_ref[j], old)
+                shift = top - bias_ref[j]
+            terms = jnp.exp2(scores - shift)
             total = jnp.sum(terms, axis=0, keepdims=True)
             moved = jnp.sum(terms * grads, axis=0, keepdims=True)
             if not first:
@@ -58,9 +106,9 @@
             mass[g] = total
             weighted[g] = moved
 
-    def backward(j, first):
-        keys = kv_ref[rows_of(j), :WIDTH]
-        values = kv_ref[rows_of(j), WIDTH:]
+    def backward(j, first, store):
+        keys = kv_all[rows_of(j), :WIDTH]
+        values = kv_all[rows_of(j), WIDTH:]
         key_grad = jnp.zeros((BLOCK, WIDTH), jnp.float32)
         value_grad = jnp.zeros((BLOCK, WIDTH), jnp.float32)
         for g in range(HEADS):
@@ -68,82 +116,215 @@
             q = q_ref[:, lanes]
             do = do_ref[:, lanes]
             scores = dot(keys, q, NT) * (factor * LOG2E)
-            probs = jnp.exp2(scores - peak[g])
+            shift = peak[g] if first else peak[g] - bias_ref[j]
+            probs = jnp.exp2(scores - shift)
             if first:
                 probs = jnp.where(causal_mask(), probs, 0.0)
             grads = dot(values, do, NT)
             dscores = (probs * ((grads - weighted[g]) * factor)).astype(jnp.bfloat16)
             value_grad = value_grad + dot(probs.astype(jnp.bfloat16), do, NN)
             key_grad = key_grad + dot(dscores, q, NN)
-            term = dot(dscores, keys, TN)
-            if first:
-                dq_acc[:, lanes] = term
-            else:
-                dq_acc[:, lanes] += term
-        dkv_ref[rows_of(j), :WIDTH] = key_grad.astype(jnp.bfloat16)
-        dkv_ref[rows_of(j), WIDTH:] = value_grad.astype(jnp.bfloat16)
+            dq_acc[:, lanes] += dot(dscores, keys, TN)
+        store(slice(0, WIDTH), key_grad)
+        store(slice(WIDTH, 2 * WIDTH), value_grad)
+
+    kv_all[rows_of(me), :] = kv_ref[...]
+    dq_acc[...] = jnp.zeros_like(dq_acc)
+    barrier = pltpu.get_barrier_semaphore()
+    for d in range(1, columns):
+        pl.semaphore_signal(
+            barrier, inc=1, device_id={"seq": z * columns + beside(d)}, device_id_type=mesh_id
+        )
+
+    @pl.when(inner)
+    def _():
+        pl.semaphore_signal(barrier, inc=1, device_id={"seq": me + columns}, device_id_type=mesh_id)
+
+    @pl.when(z > 0)
+    def _():
+        pl.semaphore_signal(barrier, inc=1, device_id={"seq": me - columns}, device_id_type=mesh_id)
+
+    pl.semaphore_wait(
+        barrier, columns - 1 + jnp.where(inner, 1, 0) + jnp.where(z > 0, 1, 0)
+    )
+
+    @pl.when(inner)
+    def _():
+        z_copy(z).start()
+
+    for d in range(1, columns):
+        @pl.when(x + d < columns)
+        def _():
+            x_copy(z, d).start()
 
     stats(me, True)
 
-    def stats_step(j, carry):
-        @pl.when(vis_ref[j] > 0)
-        def _():
+    def stats_step(i, carry):
+        level = z - 1 - i
+        wait_block(level * columns + x)
+
+        @pl.when(inner)
+        def _():
+            z_copy(level).start()
+
+        for d in range(1, columns):
+            x_copy(level, d).start()
+        stats(level * columns + x, False)
+
+        def one(d, inner_carry):
+            j = level * columns + before(d)
+            wait_block(j)
             stats(j, False)
-
-        return carry
-
-    lax.fori_loop(0, me, stats_step, 0)
+            return inner_carry
+
+        return lax.fori_loop(1, columns, one, carry)
+
+    def own_level(d, carry):
+        wait_block(me - d)
+        stats(me - d, False)
+        return carry
+
+    lax.fori_loop(1, x + 1, own_level, 0)
+    lax.fori_loop(0, z, stats_step, 0)
     for g in range(HEADS):
         weighted[g] = weighted[g] / mass[g]
         peak[g] = peak[g] + jnp.log2(mass[g])
-    backward(me, True)
-
-    def grad_step(j, carry):
-        seen = (vis_ref[j] > 0) & (j < me)
-
-        @pl.when(seen)
-        def _():
-            backward(j, False)
-
-        @pl.when(jnp.logical_not(seen) & (j != me))
-        def _():
-            dkv_ref[rows_of(j), :] = jnp.zeros((BLOCK, 2 * WIDTH), jnp.bfloat16)
-
-        return carry
-
-    lax.fori_loop(0, blocks, grad_step, 0)
+
+    def store_col(level):
+        def store(lanes, value):
+            col[level, :, lanes] = value
+
+        return store
+
+    def send_peer(level, d):
+        def store(lanes, value):
+            peer_out[level, d - 1, :, lanes] = value.astype(jnp.bfloat16)
+
+        backward(level * columns + beside(d), False, store)
+        peer_copy(level, d).start()
+
+    def add_up(level):
+        @pl.when(inner)
+        def _():
+            up_copy(level).wait_recv()
+            col[level] += up_in[level].astype(jnp.float32)
+
+    def combine(level):
+        for d in range(1, columns):
+            peer_copy(level, d).wait_recv()
+            col[level] += peer_in[level, d - 1].astype(jnp.float32)
+        add_up(level)
+        up_out[level] = col[level].astype(jnp.bfloat16)
+        up_copy(level).start()
+
+    def grad_step(level, carry):
+        def one(d, inner_carry):
+            send_peer(level, d)
+            return inner_carry
+
+        lax.fori_loop(1, columns, one, 0)
+        backward(level * columns + x, False, store_col(level))
+
+        @pl.when(level > 0)
+        def _():
+            combine(level - 1)
+
+        return carry
+
+    lax.fori_loop(0, z, grad_step, 0)
+
+    def own_peer(d, carry):
+        send_peer(z, d)
+        return carry
+
+    lax.fori_loop(columns - x, columns, own_peer, 0)
+
+    @pl.when(z > 0)
+    def _():
+        combine(z - 1)
+
+    backward(me, True, store_col(z))
     dq_ref[...] = dq_acc[...].astype(jnp.bfloat16)
-
-
-def attention(visible, q, do, kv):
-    window = kv.shape[0]
+    for d in range(1, columns):
+        @pl.when(d > x)
+        def _():
+            peer_copy(z, d).wait_recv()
+            col[z] += peer_in[z, d - 1].astype(jnp.float32)
+
+    add_up(z)
+    dkv_ref[...] = col[z].astype(jnp.bfloat16)
+
+    def drain(level, carry):
+        @pl.when(inner)
+        def _():
+            z_copy(level).wait_send()
+
+        @pl.when(level < z)
+        def _():
+            up_copy(level).wait_send()
+
+        for d in range(1, columns):
+            @pl.when((level < z) | (x + d < columns))
+            def _():
+                x_copy(level, d).wait_send()
+
+            @pl.when((level < z) | (x + d >= columns))
+            def _():
+                peer_copy(level, d).wait_send()
+
+        return carry
+
+    lax.fori_loop(0, z + 1, drain, 0)
+
+
+def attention(blocks, bias, q, do, kv):
+    window = blocks * BLOCK
+    levels = 4
+    columns = blocks // levels
     vmem = pl.BlockSpec(memory_space=pltpu.VMEM)
     pairs = HEADS * BLOCK * BLOCK * 7
+    pair = (BLOCK, 2 * WIDTH)
+    bf16, f32, dma = jnp.bfloat16, jnp.float32, pltpu.SemaphoreType.DMA
     return pl.pallas_call(
-        attention_kernel,
+        functools.partial(attention_kernel, columns),
         out_shape=(
-            jax.ShapeDtypeStruct((BLOCK, HEADS * WIDTH), jnp.bfloat16),
-            jax.ShapeDtypeStruct((window, 2 * WIDTH), jnp.bfloat16),
+            jax.ShapeDtypeStruct((BLOCK, HEADS * WIDTH), bf16),
+            jax.ShapeDtypeStruct(pair, bf16),
         ),
-        in_specs=[pl.BlockSpec(memory_space=pltpu.SMEM), vmem, vmem, vmem],
+        in_specs=[vmem, vmem, vmem, vmem],
         out_specs=(vmem, vmem),
         scratch_shapes=[
-            pltpu.VMEM((BLOCK, HEADS * WIDTH), jnp.float32),
-            pltpu.VMEM((HEADS, 1, BLOCK), jnp.float32),
-            pltpu.VMEM((HEADS, 1, BLOCK), jnp.float32),
-            pltpu.VMEM((HEADS, 1, BLOCK), jnp.float32),
+            pltpu.VMEM((window, 2 * WIDTH), bf16),
+            pltpu.VMEM((BLOCK, HEADS * WIDTH), f32),
+            pltpu.VMEM((HEADS, 1, BLOCK), f32),
+            pltpu.VMEM((HEADS, 1, BLOCK), f32),
+            pltpu.VMEM((HEADS, 1, BLOCK), f32),
+            pltpu.VMEM((levels,) + pair, f32),
+            pltpu.VMEM((levels, columns - 1) + pair, bf16),
+            pltpu.VMEM((levels, columns - 1) + pair, bf16),
+            pltpu.VMEM((levels,) + pair, bf16),
+            pltpu.VMEM((levels,) + pair, bf16),
+            dma((blocks,)),
+            dma((levels,)),
+            dma((levels, columns - 1)),
+            dma((levels, columns - 1)),
+            dma((levels, columns - 1)),
+            dma((levels,)),
+            dma((levels,)),
         ],
-        compiler_params=pltpu.CompilerParams(vmem_limit_bytes=48 * 2**20),
+        compiler_params=pltpu.CompilerParams(
+            collective_id=2, has_side_effects=True, vmem_limit_bytes=48 * 2**20
+        ),
         cost_estimate=pl.CostEstimate(
             flops=7 * 2 * pairs * WIDTH, bytes_accessed=6 * 2**20, transcendentals=2 * pairs
         ),
         name="attention",
-    )(visible, q, do, kv)
+    )(bias, q, do, kv)
 
 
 def project_kernel(
     size, chunks, dq_ref, dkv_ref, wq_ref, wk_ref, wv_ref, out_ref,
-    rows_all, weights, product, own, core_out, core_in, far_out, far_in,
+    rows_all, mixed, wide, weights, product, own, core_out, core_in, far_out, far_in,
     w_sem, core_send, core_recv, far_send, far_recv,
 ):
     me = lax.axis_index("kvh")
@@ -151,14 +332,17 @@
     core = me % 2
     layers = size // 2
     rows = BLOCK // size
-    width = wq_ref.shape[0] // chunks
+    width = wk_ref.shape[0] // chunks
     qw = HEADS * WIDTH
     peer = layer * 2 + 1 - core
 
     def weight_copies(i):
         at = pl.ds(pl.multiple_of(i * width, width), width)
         return [
-            pltpu.make_async_copy(wq_ref.at[at, :], weights.at[i, :, pl.ds(0, qw)], w_sem.at[i, 0]),
+            pltpu.make_async_copy(
+                wq_ref.at[pl.ds(pl.multiple_of(i * width * HEADS, width * HEADS), width * HEADS), :],
+                mixed.at[i], w_sem.at[i, 0],
+            ),
             pltpu.make_async_copy(wk_ref.at[at, :], weights.at[i, :, pl.ds(qw, WIDTH)], w_sem.at[i, 1]),
             pltpu.make_async_copy(
                 wv_ref.at[at, :], weights.at[i, :, pl.ds(qw + WIDTH, WIDTH)], w_sem.at[i, 2]
@@ -201,6 +385,9 @@
         for copy in weight_copies(i):
             copy.wait()
         slot = i % 2
+        wide[...] = mixed[i].astype(jnp.float32)
+        for g in range(HEADS):
+            weights[i, :, g * WIDTH:(g + 1) * WIDTH] = wide[pl.ds(g, width, HEADS), :].astype(jnp.bfloat16)
         product[slot] = dot(rows_all[...], weights[i], NT)
         for d in list(range(1, layers)) + [0]:
             core_out[d, i] = product[slot, part(d, 1 - core), :].astype(jnp.bfloat16)
@@ -243,7 +430,7 @@
 
 
 def project(size, dq, dkv, wq, wk, wv):
-    model = wq.shape[0]
+    model = wk.shape[0]
     rows = BLOCK // size
     layers = size // 2
     chunks = 16
@@ -258,6 +445,8 @@
         out_specs=vmem,
         scratch_shapes=[
             pltpu.VMEM((BLOCK, full), jnp.bfloat16),
+            pltpu.VMEM((chunks, width * HEADS, WIDTH), jnp.bfloat16),
+            pltpu.VMEM((width * HEADS, WIDTH), jnp.float32),
             pltpu.VMEM((chunks, width, full), jnp.bfloat16),
             pltpu.VMEM((2, BLOCK, width), jnp.float32),
             pltpu.VMEM((chunks, rows, width), jnp.float32),
@@ -288,17 +477,17 @@
     q = queries.reshape(BLOCK, HEADS * WIDTH)
     do = grad_out.reshape(BLOCK, HEADS * WIDTH)
     kv = jnp.concatenate([key_states[:, 0], value_states[:, 0]], 1)
-    gathered = lax.all_gather(kv, "seq", axis=0, tiled=True)
     blocks = ancestors.shape[0]
     me = lax.axis_index("seq")
     listed = lax.dynamic_index_in_dim(ancestors, me, 0, keepdims=False)
     ids = jnp.arange(blocks, dtype=jnp.int32)
-    visible = jnp.any(listed[None, :] == ids[:, None], axis=1).astype(jnp.int32)
-    dq, dkv = attention(visible, q, do, gathered)
-    pair = lax.psum_scatter(dkv, "seq", scatter_dimension=0, tiled=True)
+    visible = jnp.any(listed[None, :] == ids[:, None], axis=1)
+    bias = jnp.where(visible, 0.0, -jnp.inf).astype(jnp.float32)
+    bias = jnp.broadcast_to(bias[:, None, None], (blocks, 1, BLOCK))
+    dq, pair = attention(blocks, bias, q, do, kv)
     grad_input = project(
         size, dq, pair,
-        query_weight.reshape(model, HEADS * WIDTH), key_weight[:, 0], value_weight[:, 0],
+        query_weight.reshape(model * HEADS, WIDTH), key_weight[:, 0], value_weight[:, 0],
     )
     return (grad_input, pair[:, None, :WIDTH], pair[:, None, WIDTH:])
 

time: 232 us -> 131 us (0.56)
  waiting for transfers between devices: 139 us -> 0 us
  Pallas kernels: 61 us -> 123 us
  between operations: 14.1 us -> 0.68 us
  local copies, waits for them, and re-layouts: 15.7 us -> 6.78 us
    reduce_scatter x1 -> x0, waiting for transfers between devices: 86.8 us -> none  [local(): pair = lax.psum_scatter(dkv, 'seq', scatter_dimension=0, tiled=True)]
    pallas_call x1, Pallas kernels: 6.85 us -> 68.5 us  [attention(): pl.pallas_call(functools.partial(attention_kernel, columns), out_shape=(j...]
    all_gather x1 -> x0, waiting for transfers between devices: 52.2 us -> none  [local(): gathered = lax.all_gather(kv, 'seq', axis=0, tiled=True)]
    unnamed x10 -> x7, local copies, waits for them, and re-layouts: 13.6 us -> 4.58 us
  transfers between devices with their start and end apart: 2 -> 0, of which waited for: 2 -> 0; matrix products, arithmetic and copies ran while one was open for 4% -> 0% of each run, Pallas kernels for 0% -> 0%
where the time goes in v2:
time: 131 us
  Pallas kernels  123 us (94%)
  local copies, waits for them, and re-layouts  6.78 us (5%)
    pallas_call x1, Pallas kernels, attention(): pl.pallas_call(functools.partial(attention_kernel, columns), out_shape=(j...  68.5 us
    pallas_call x1, Pallas kernels, project(): pl.pallas_call(functools.partial(project_kernel, size, chunks), out_shape...  54.3 us
    unnamed x7, local copies, waits for them, and re-layouts  4.58 us

profile of v2, /device:TPU:0, one launch (start us, length us, event | category | flops | bytes accessed | tf_op | source)
XLA Modules:
  0.0 131.3 jit_solution(4877738591382955475)
XLA Ops:
  0.6 0.0 copy-start
  0.6 0.7 copy-done
  1.3 0.1 fusion
  1.5 0.1 broadcast_in_dim.24.bias_ref
  1.5 1.0 pad_maximum_fusion.kv_ref
  2.5 1.4 %copy_bitcast_fusion = (bf16[512,512]{1,0:T(8,128)(2,1)S(1)}, bf16[512,512]{1,0:T(8,128)(2,1)S(1)}) fusion(bf16[64,8,4,128]{3,2,1,0:T(4,128)(2,1)} %bitcast.19, bf16[64,8,4,128]{3,2,1,0:T(4,128)(2,1)} %bitcast.20), kind=kLoop, calls=%fused_computation | loop fusion | bytes 2097152 | tf_op jit(solution)/shard_map/reshape | solution.py:478
  3.9 68.5 %attention.1 = (bf16[512,512]{1,0:T(8,128)(2,1)S(1)}, bf16[512,256]{1,0:T(8,128)(2,1)S(1)}) custom-call(f32[8,1,512]{2,1,0:T(1,128)S(1)} %broadcast_in_dim.24.bias_ref, bf16[512,512]{1,0:T(8,128)(2,1)S(1)} %get-tuple-element.10.q_ref, bf16[512,512]{1,0:T(8,128)(2,1)S(1)} %get-tuple-element.9.do_ref, bf16[512,256]{1,0:T(8,128)(2,1)S(1)} %pad_maximum_fusion.kv_ref), custom_call_target="tpu_custom_call" | custom-call | flops 13153337344 | bytes 6291456 | tf_op jit(solution)/shard_map/attention/pallas_call | solution.py:288
  72.4 0.0 copy-start.2
  72.4 0.8 copy-done.2
  73.1 0.0 copy-start.1
  73.2 0.8 slice_bitcast_fusion
  73.9 0.0 copy-done.1
  73.9 54.3 %project.1 = bf16[128,8192]{1,0:T(8,128)(2,1)} custom-call(bf16[512,512]{1,0:T(8,128)(2,1)} %copy-done.2, bf16[512,256]{1,0:T(8,128)(2,1)} %copy-done.1, bf16[32768,128]{1,0:T(8,128)(2,1)} %bitcast.23, bf16[8192,128]{1,0:T(8,128)(2,1)} %bitcast.24, bf16[8192,128]{1,0:T(8,128)(2,1)} %bitcast.25), custom_call_target="tpu_custom_call" | custom-call | flops 6442450944 | bytes 12582912 | tf_op jit(solution)/shard_map/project/pallas_call | solution.py:441
  128.2 3.1 %copy.16 = bf16[128,8192]{1,0:T(8,128)(2,1)} copy(bf16[128,8192]{1,0:T(8,128)(2,1)} %project.1) | data formatting | bytes 4194304
  (2 shorter events, 0.0 us)
Async XLA Ops:
  0.6 0.7 copy-start
  72.4 0.8 copy-start.2
  73.1 0.8 copy-start.1
